TPU v7x, 512 devices: a whole 4x4x16 slice. The times are simulated.
512 devices in a mesh: oct: 32 (over z, core), dev: 16 (over y, x).
Axes of the slice: x: 4, y: 4, z: 16, core: 2. Of those that a mesh axis runs over, the one named last changes fastest.
Arguments:
- leaf_multipoles: float32 [32768, 512], P(('oct', 'dev')), may hold values from -6 to 6
- m2l_ops: bfloat16 [316, 96, 96], P(None, 'dev'), may hold values from -0.046875 to 0.046875
- compress: float32 [512, 96], replicated, may hold values from -0.25 to 0.25
- expand: float32 [96, 512], replicated, may hold values from -0.625 to 0.625
Outputs:
- leaf_locals: float32 [32768, 512], P(('oct', 'dev'))
All inputs are finite; a program needn't handle non-finite values.
Results may differ from a plain program's by a relative error of at most 0.0029.
Values may be sent and summed in bfloat16 or wider, within the bound.
A program may use at most 64 MiB of HBM per device.

v0:
```python
import math

import jax
import jax.numpy as jnp
import numpy as np
from jax import lax
from jax.sharding import PartitionSpec as P

ORDER = 8
COEF = 512
RANK = 96
CUBE = 4


def shortened(value):

    def short(part):
        return part.astype(jnp.bfloat16) if part.dtype == jnp.float32 else part

    return jax.tree.map(short, value)


def from_behind(value, axis, steps):
    count = lax.axis_size(axis)
    initial, last = (max(0, -steps), min(count, count - steps))
    return lax.ppermute(value, axis, [(source, source + steps) for source in range(initial, last)])


def offset_table():
    entries = []
    for step_z in range(-3, 4):
        for step_y in range(-3, 4):
            for step_x in range(-3, 4):
                if max(abs(step_z), abs(step_y), abs(step_x)) > 1:
                    entries.append((step_z, step_y, step_x))
    return entries


def parity_table():
    entries = []
    for octant_code in range(8):
        parity = (octant_code // 4, octant_code // 2 % 2, octant_code % 2)
        entry_list = []
        for offset_key in offset_table():
            allowed = all(
                (
                    -2 - parity[axis_id] <= offset_key[axis_id] <= 3 - parity[axis_id]
                    for axis_id in range(3)
                )
            )
            entry_list.append(1.0 if allowed else 0.0)
        entries.append(entry_list)
    return np.array(entries, dtype=np.float32)


def plane_masks(side_cells):
    table_rows = parity_table()
    masks = np.zeros((2, side_cells, side_cells, table_rows.shape[1]), dtype=np.float32)
    for parity_z in range(2):
        for index_y in range(side_cells):
            for index_x in range(side_cells):
                masks[parity_z, index_y, index_x] = table_rows[
                    parity_z * 4 + index_y % 2 * 2 + index_x % 2
                ]
    return masks


def child_maps(node_count):
    node_ids = jnp.arange(node_count, dtype=jnp.float32)
    angles = (2.0 * node_ids + 1.0) * math.pi / (2.0 * node_count)
    points = jnp.cos(angles)
    degrees = jnp.arange(1, node_count, dtype=jnp.float32)
    parent_poly = jnp.cos(angles[:, None] * degrees[None, :])
    matrices = []
    for child_side in range(2):
        shifted = (points + (2.0 * child_side - 1.0)) / 2.0
        child_poly = jnp.cos(jnp.arccos(shifted)[:, None] * degrees[None, :])
        products = jnp.sum(parent_poly[:, None, :] * child_poly[None, :, :], axis=-1)
        matrices.append(1.0 / node_count + 2.0 / node_count * products)
    return jnp.stack(matrices)


def octant_tables(node_count):
    side_maps = child_maps(node_count)
    along_z = jnp.stack([side_maps[octant // 4] for octant in range(8)])
    pair_maps = []
    for octant in range(8):
        tensor = (
            side_maps[octant // 2 % 2][:, None, :, None] * side_maps[octant % 2][None, :, None, :]
        )
        pair_maps.append(tensor.reshape(node_count * node_count, node_count * node_count))
    return (along_z, jnp.stack(pair_maps))


def lift(children, tables):
    mixed = jnp.einsum("qpij,qlj->qpil", children, tables[1], precision=lax.Precision.HIGHEST)
    return jnp.einsum("qpil,qai->pal", mixed, tables[0], precision=lax.Precision.HIGHEST)


def lower(parents, tables):
    mixed = jnp.einsum("pal,qai->qpil", parents, tables[0], precision=lax.Precision.HIGHEST)
    return jnp.einsum("qpil,qlj->qpij", mixed, tables[1], precision=lax.Precision.HIGHEST)


def lift_grid(grid_values, tables):
    node_count = tables[0].shape[1]
    size_z, size_y, size_x, coef_count = grid_values.shape
    grouped = grid_values.reshape(size_z // 2, 2, size_y // 2, 2, size_x // 2, 2, coef_count)
    grouped = grouped.transpose(1, 3, 5, 0, 2, 4, 6).reshape(
        8, -1, node_count, node_count * node_count
    )
    return lift(grouped, tables).reshape(size_z // 2, size_y // 2, size_x // 2, coef_count)


def lower_grid(grid_values, tables):
    node_count = tables[0].shape[1]
    size_z, size_y, size_x, coef_count = grid_values.shape
    spread = lower(grid_values.reshape(-1, node_count, node_count * node_count), tables)
    spread = spread.reshape(2, 2, 2, size_z, size_y, size_x, coef_count).transpose(
        3, 0, 4, 1, 5, 2, 6
    )
    return spread.reshape(2 * size_z, 2 * size_y, 2 * size_x, coef_count)


def compress_rows(grid_values, compress):
    flat_rows = jnp.dot(
        grid_values.reshape(-1, grid_values.shape[-1]),
        compress,
        precision=lax.Precision.HIGHEST,
        preferred_element_type=jnp.float32,
    )
    return flat_rows.astype(jnp.bfloat16).reshape(grid_values.shape[:-1] + (compress.shape[1],))


def expand_rows(grid_values, expand):
    flat_rows = jnp.dot(
        grid_values.reshape(-1, grid_values.shape[-1]),
        expand,
        precision=lax.Precision.HIGHEST,
        preferred_element_type=jnp.float32,
    )
    return flat_rows.reshape(grid_values.shape[:-1] + (expand.shape[1],))


def fetch_near(piece_cells, shift_by):
    return from_behind(shortened(piece_cells), ("oct", "dev"), shift_by).astype(piece_cells.dtype)


def axis_halo(block_cells, coords, extents, strides):
    reach_cells = 2
    for axis_id in range(3):
        side_cells = block_cells.shape[axis_id]
        hop_total = -(-reach_cells // side_cells)
        lower_parts = []
        upper_parts = []
        for distance in range(1, hop_total + 1):
            cell_count = min(reach_cells - (distance - 1) * side_cells, side_cells)
            tail_cells = lax.slice_in_dim(
                block_cells, side_cells - cell_count, side_cells, axis=axis_id
            )
            head_cells = lax.slice_in_dim(block_cells, 0, cell_count, axis=axis_id)
            from_below = fetch_near(tail_cells, distance * strides[axis_id])
            from_below = jnp.where(
                coords[axis_id] >= distance, from_below, jnp.zeros_like(from_below)
            )
            from_above = fetch_near(head_cells, -distance * strides[axis_id])
            from_above = jnp.where(
                coords[axis_id] + distance < extents[axis_id],
                from_above,
                jnp.zeros_like(from_above),
            )
            lower_parts.insert(0, from_below)
            upper_parts.append(from_above)
        block_cells = jnp.concatenate(lower_parts + [block_cells] + upper_parts, axis=axis_id)
    return block_cells


def plane_rows(wide_cells, side_cells, masks, weight_rows):
    offsets = offset_table()

    def one_plane(target_z):
        window = lax.dynamic_slice_in_dim(wide_cells, target_z, 7, axis=0)
        pieces = [
            window[
                3 + key[0],
                3 + key[1] : 3 + key[1] + side_cells,
                3 + key[2] : 3 + key[2] + side_cells,
            ]
            for key in offsets
        ]
        stacked = jnp.stack(pieces, axis=2)
        keep_mask = lax.dynamic_index_in_dim(masks, target_z % 2, 0, keepdims=False)
        stacked = stacked * keep_mask[..., None]
        return jnp.dot(
            stacked.reshape(side_cells * side_cells, -1),
            weight_rows,
            preferred_element_type=jnp.float32,
        )

    return lax.map(one_plane, jnp.arange(side_cells, dtype=jnp.int32))


def single_row(padded_grid, position, keep_row, window_ids):
    rank_width = padded_grid.shape[-1]
    anchor = jnp.zeros((), jnp.int32)
    starts = tuple((place.astype(jnp.int32) for place in position))
    window = lax.dynamic_slice(padded_grid, starts + (anchor,), (7, 7, 7, rank_width))
    chosen = jnp.take(window.reshape(343, rank_width), window_ids, axis=0)
    return (chosen * keep_row[:, None]).reshape(1, -1)


def on_device(leaf_multipoles, m2l_ops, compress, expand):
    tables = octant_tables(ORDER)
    across_x = min(8, lax.axis_size("dev"))
    across_z = lax.axis_size("oct") * lax.axis_size("dev") // (across_x * across_x)
    device = lax.axis_index(("oct", "dev"))
    coord_x = device % across_x
    coord_y = device // across_x % across_x
    coord_z = device // (across_x * across_x)
    coords = (coord_z, coord_y, coord_x)
    extents = (across_z, across_x, across_x)
    strides = (across_x * across_x, across_x, 1)
    parents = (coord_z // 2, coord_y // 2, coord_x // 2)
    octant = coord_z % 2 * 4 + coord_y % 2 * 2 + coord_x % 2
    parent_octant = parents[0] % 2 * 4 + parents[1] % 2 * 2 + parents[2] % 2
    level_five = leaf_multipoles.reshape(CUBE, CUBE, CUBE, COEF)
    level_four = lift_grid(level_five, tables)
    own_top = lift_grid(level_four, tables).reshape(1, COEF)
    everyone = lax.all_gather(own_top, ("oct", "dev"), axis=0, tiled=True)
    level_three = everyone.reshape(across_z, across_x, across_x, COEF)
    packed_three = compress_rows(level_three, compress)
    packed_two = compress_rows(lift_grid(level_three, tables), compress)
    packed_five = compress_rows(level_five, compress)
    packed_four = compress_rows(level_four, compress)
    wide_five = axis_halo(packed_five, coords, extents, strides)
    wide_four = axis_halo(packed_four, coords, extents, strides)
    rim_one = ((1, 1), (1, 1), (1, 1), (0, 0))
    rim_three = ((3, 3), (3, 3), (3, 3), (0, 0))
    wide_five = jnp.pad(wide_five, rim_one)
    wide_four = jnp.pad(wide_four, rim_one)
    padded_three = jnp.pad(packed_three, rim_three)
    padded_two = jnp.pad(packed_two, rim_three)
    window_ids = jnp.asarray(
        np.array(
            [(key[0] + 3) * 49 + (key[1] + 3) * 7 + key[2] + 3 for key in offset_table()],
            dtype=np.int32,
        )
    )
    parity_rows = jnp.asarray(parity_table()).astype(jnp.bfloat16)
    keep_three = lax.dynamic_index_in_dim(parity_rows, octant, 0, keepdims=False)
    keep_two = lax.dynamic_index_in_dim(parity_rows, parent_octant, 0, keepdims=False)
    five_masks = jnp.asarray(plane_masks(CUBE)).astype(jnp.bfloat16)
    four_masks = jnp.asarray(plane_masks(CUBE // 2)).astype(jnp.bfloat16)
    start_totals = (
        jnp.zeros((CUBE, CUBE * CUBE, RANK), jnp.float32),
        jnp.zeros((CUBE // 2, CUBE // 2 * (CUBE // 2), RANK), jnp.float32),
        jnp.zeros((2, RANK), jnp.float32),
    )
    piece = jax.tree.map(lambda part: lax.all_gather(part, "dev", axis=1, tiled=True), m2l_ops)
    rank_width = piece.shape[1]
    weight_rows = piece.reshape(-1, piece.shape[2])

    def rank_cut(values):
        return lax.slice_in_dim(values, 0, rank_width, axis=3)

    near_five = plane_rows(rank_cut(wide_five), CUBE, five_masks, weight_rows)
    near_four = plane_rows(rank_cut(wide_four), CUBE // 2, four_masks, weight_rows)
    top_rows = jnp.concatenate(
        [
            single_row(rank_cut(padded_three), coords, keep_three, window_ids),
            single_row(rank_cut(padded_two), parents, keep_two, window_ids),
        ],
        axis=0,
    )
    near_top = jnp.dot(top_rows, weight_rows, preferred_element_type=jnp.float32)
    near_five, near_four, near_top = (
        start_totals[0] + near_five,
        start_totals[1] + near_four,
        start_totals[2] + near_top,
    )
    local_two = expand_rows(near_top[1:2] * 0.125, expand)
    spread = lower(local_two.reshape(1, ORDER, ORDER * ORDER), tables)
    local_three = lax.dynamic_index_in_dim(spread, octant, 0, keepdims=False).reshape(1, COEF)
    local_three = local_three + expand_rows(near_top[0:1] * 0.25, expand)
    local_four = lower_grid(local_three.reshape(1, 1, 1, COEF), tables)
    local_four = local_four + expand_rows(
        near_four.reshape(CUBE // 2, CUBE // 2, CUBE // 2, RANK) * 0.5, expand
    )
    local_five = lower_grid(local_four, tables) + expand_rows(
        near_five.reshape(CUBE, CUBE, CUBE, RANK), expand
    )
    return local_five.reshape(-1, COEF)


def solution(mesh):
    placed = (P(("oct", "dev"), None), P(None, "dev", None), P(), P())
    return jax.shard_map(
        on_device, mesh=mesh, in_specs=placed, out_specs=P(("oct", "dev"), None), check_vma=False
    )
```

profile of v0, /device:TPU:1, one launch (start us, length us, event | category | flops | bytes accessed | tf_op | source)
XLA Modules:
  0.0 432.0 jit_solution(17079386888209924408)
XLA Ops:
  14.5 6.4 %collective-permute-start = (bf16[2,2,2,96]{3,2,1,0:T(2,128)(2,1)S(1)}, bf16[2,2,2,96]{3,2,1,0:T(2,128)(2,1)S(1)}, u32[]{:S(2)}, u32[]{:S(2)}) collective-permute-start(bf16[2,2,2,96]{3,2,1,0:T(2,128)(2,1)S(1)} %bitcast.3838), channel_id=1, source_target_pairs={{0,64},{1,65},{2,66},{3,67},{4,68},{5,69},{6,70},{7,71},{8,72},{9,... | collective-permute-start | bytes 4616 | tf_op jit(solution)/shard_map/ppermute | solution.py:26
  22.5 6.7 %collective-permute-start.6 = (bf16[2,4,4,96]{3,2,1,0:T(4,128)(2,1)S(1)}, bf16[2,4,4,96]{3,2,1,0:T(4,128)(2,1)S(1)}, u32[]{:S(2)}, u32[]{:S(2)}) collective-permute-start(bf16[2,4,4,96]{3,2,1,0:T(4,128)(2,1)S(1)} %bitcast.3846), channel_id=1, source_target_pairs={{0,64},{1,65},{2,66},{3,67},{4,68},{5,69},{6,70},{7,71},{8,72},{9,... | collective-permute-start | bytes 18440 | tf_op jit(solution)/shard_map/ppermute | solution.py:26
  30.6 5.9 %collective-permute-start.3 = (bf16[6,2,2,96]{3,2,1,0:T(2,128)(2,1)S(1)}, bf16[6,2,2,96]{3,2,1,0:T(2,128)(2,1)S(1)}, u32[]{:S(2)}, u32[]{:S(2)}) collective-permute-start(bf16[6,2,2,96]{3,2,1,0:T(2,128)(2,1)S(1)} %pad_maximum_fusion.3), channel_id=1, source_target_pairs={{8,0},{9,1},{10,2},{11,3},{12,4},{13,5},{14,6},{15,7},{16,8},{17,9... | collective-permute-start | bytes 13832 | tf_op jit(solution)/shard_map/ppermute | solution.py:26
  38.6 5.7 %collective-permute-start.9 = (bf16[8,2,4,96]{3,2,1,0:T(4,128)(2,1)S(1)}, bf16[8,2,4,96]{3,2,1,0:T(4,128)(2,1)S(1)}, u32[]{:S(2)}, u32[]{:S(2)}) collective-permute-start(bf16[8,2,4,96]{3,2,1,0:T(4,128)(2,1)S(1)} %get-tuple-element.335), channel_id=1, source_target_pairs={{8,0},{9,1},{10,2},{11,3},{12,4},{13,5},{14,6},{15,7},{16,8},{17,9... | collective-permute-start | bytes 36872 | tf_op jit(solution)/shard_map/ppermute | solution.py:26
  44.4 4.9 %collective-permute-start.5 = (bf16[6,6,2,96]{3,2,1,0:T(2,128)(2,1)S(1)}, bf16[6,6,2,96]{3,2,1,0:T(2,128)(2,1)S(1)}, u32[]{:S(2)}, u32[]{:S(2)}) collective-permute-start(bf16[6,6,2,96]{3,2,1,0:T(2,128)(2,1)S(1)} %pad_maximum_fusion.2), channel_id=1, source_target_pairs={{1,0},{2,1},{3,2},{4,3},{5,4},{6,5},{7,6},{8,7},{9,8},{10,9},{11,1... | collective-permute-start | bytes 41480 | tf_op jit(solution)/shard_map/ppermute | solution.py:26
  54.0 3.8 collective-permute-done.8
  58.0 7.5 %collective-permute-start.11 = (bf16[8,8,2,96]{3,2,1,0:T(2,128)(2,1)S(1)}, bf16[8,8,2,96]{3,2,1,0:T(2,128)(2,1)S(1)}, u32[]{:S(2)}, u32[]{:S(2)}) collective-permute-start(bf16[8,8,2,96]{3,2,1,0:T(2,128)(2,1)S(1)} %get-tuple-element.333), channel_id=1, source_target_pairs={{1,0},{2,1},{3,2},{4,3},{5,4},{6,5},{7,6},{8,7},{9,8},{10,9},{11,1... | collective-permute-start | bytes 73736 | tf_op jit(solution)/shard_map/ppermute | solution.py:26
  67.7 6.4 %collective-permute-done.10 = bf16[8,8,2,96]{3,2,1,0:T(2,128)(2,1)S(1)} collective-permute-done((bf16[8,8,2,96]{3,2,1,0:T(2,128)(2,1)S(1)}, bf16[8,8,2,96]{3,2,1,0:T(2,128)(2,1)S(1)}, u32[]{:S(2)}, u32[]{:S(2)}) %collective-permute-start.10) | collective-permute-done | bytes 24608 | tf_op jit(solution)/shard_map/ppermute | solution.py:26
  74.4 111.1 %all-gather.6.cloned.1.call-done = f32[512,1,512]{2,1,0:T(1,128)} async-done(((f32[1,1,512]{2,1,0:T(1,128)}), f32[512,1,512]{2,1,0:T(1,128)}) %all-gather.6.cloned.1.call-update) | async-done | bytes 1048592 | tf_op jit(solution)/shard_map/all_gather | solution.py:229
  185.5 3.7 reduce.1
  195.5 4.5 %fusion.640 = f32[64,8,64]{2,1,0:T(8,128)S(1)} fusion(f32[8,64,8,64]{3,1,2,0:T(8,128)S(1)} %fusion.638, f32[8,8,8]{0,1,2:T(8,128)S(1)} %stack.20), kind=kOutput, calls=%fused_computation.1919 | convolution fusion | flops 25165824 | bytes 1181696 | tf_op jit(solution)/shard_map/qpil,qai->pal/dot_general | solution.py:97
  205.9 58.1 %all-gather.4.cloned.1.call-done = bf16[316,96,96]{0,2,1:T(8,128)(2,1)} async-done(((bf16[316,6,96]{0,2,1:T(8,128)(2,1)}), bf16[316,96,96]{0,2,1:T(8,128)(2,1)}) %all-gather.4.cloned.1.call-update) | async-done | bytes 5824528 | tf_op jit(solution)/shard_map/all_gather | solution.py:259
  264.0 11.5 %copy.131 = bf16[316,96,96]{1,0,2:T(8,128)(2,1)} copy(bf16[316,96,96]{0,2,1:T(8,128)(2,1)} %all-gather.4.cloned.1.call-done) | data formatting | bytes 11649024 | tf_op jit(solution)/shard_map/all_gather | solution.py:259
  275.5 14.9 %reshape.389 = bf16[30336,96]{0,1:T(8,128)(2,1)} reshape(bf16[316,96,96]{1,0,2:T(8,128)(2,1)} %copy.131) | data formatting | bytes 11649024 | tf_op jit(solution)/shard_map/reshape | solution.py:261
  290.4 9.6 %copy.135 = bf16[30336,96]{1,0:T(8,128)(2,1)} copy(bf16[30336,96]{0,1:T(8,128)(2,1)} %reshape.389) | data formatting | bytes 11649024 | tf_op jit(solution)/shard_map/while | solution.py:200
  300.0 4.3 fusion.700
  306.5 33.6 %while.24 = (s32[]{:T(128)}, f32[2,4,96]{2,1,0:T(4,128)S(1)}, s32[2]{0:T(128)S(1)}, bf16[8,8,8,96]{3,2,1,0:T(8,128)(2,1)S(1)}, bf16[2,2,2,316]{3,2,1,0:T(2,128)(...) while((s32[]{:T(128)}, f32[2,4,96]{2,1,0:T(4,128)S(1)}, ...), condition=%wide.region_3.5_spmd, body=%wide.region_2.4_spmd.sunk | while | flops 23540764 | bytes 8188561 | solution.py:200
  319.0 4.3 %fusion.773 = f32[2,4,96]{2,1,0:T(4,128)S(1)} fusion(f32[2,4,96]{2,1,0:T(4,128)S(1)} %get-tuple-element.674, s32[]{:T(128)S(6)} %copy.812, bf16[4,30336]{1,0:T(4,128)(2,1)S(1)} %mul.462, bf16[30336,96]{1,0:T(8,128)(2,1)} %get-tuple-element.694), kind=kOutput, calls=%fused_computation.3.clone.1 | convolution fusion | flops 23298048 | bytes 6069252 | tf_op jit(solution)/shard_map/while/body/eval_jaxpr/dot_general | solution.py:194
  335.8 4.3 %fusion.773 = f32[2,4,96]{2,1,0:T(4,128)S(1)} fusion(f32[2,4,96]{2,1,0:T(4,128)S(1)} %get-tuple-element.674, s32[]{:T(128)S(6)} %copy.812, bf16[4,30336]{1,0:T(4,128)(2,1)S(1)} %mul.462, bf16[30336,96]{1,0:T(8,128)(2,1)} %get-tuple-element.694), kind=kOutput, calls=%fused_computation.3.clone.1 | convolution fusion | flops 23298048 | bytes 6069252 | tf_op jit(solution)/shard_map/while/body/eval_jaxpr/dot_general | solution.py:194
  341.6 82.3 %while.25 = (s32[]{:T(128)}, f32[4,16,96]{2,1,0:T(8,128)S(1)}, s32[4]{0:T(128)S(1)}, bf16[10,10,10,96]{3,2,1,0:T(8,128)(2,1)S(1)}, bf16[2,4,4,316]{3,2,1,0:T(4,1...) while((s32[]{:T(128)}, f32[4,16,96]{2,1,0:T(8,128)S(1)}, ...), condition=%wide.region_5.7_spmd, body=%wide.region_4.6_spmd.sunk | while | flops 94162976 | bytes 15269809 | solution.py:200
  357.9 4.4 %fusion.777 = f32[4,16,96]{2,1,0:T(8,128)S(1)} fusion(f32[4,16,96]{2,1,0:T(8,128)S(1)} %get-tuple-element.722, s32[]{:T(128)S(6)} %copy.818, bf16[16,30336]{1,0:T(8,128)(2,1)S(1)} %mul.465, bf16[30336,96]{1,0:T(8,128)(2,1)} %get-tuple-element.742), kind=kOutput, calls=%fused_computation.957.clone.1 | convolution fusion | flops 93192192 | bytes 6803460 | tf_op jit(solution)/shard_map/while/body/eval_jaxpr/dot_general | solution.py:194
  378.5 4.4 %fusion.777 = f32[4,16,96]{2,1,0:T(8,128)S(1)} fusion(f32[4,16,96]{2,1,0:T(8,128)S(1)} %get-tuple-element.722, s32[]{:T(128)S(6)} %copy.818, bf16[16,30336]{1,0:T(8,128)(2,1)S(1)} %mul.465, bf16[30336,96]{1,0:T(8,128)(2,1)} %get-tuple-element.742), kind=kOutput, calls=%fused_computation.957.clone.1 | convolution fusion | flops 93192192 | bytes 6803460 | tf_op jit(solution)/shard_map/while/body/eval_jaxpr/dot_general | solution.py:194
  399.0 4.4 %fusion.777 = f32[4,16,96]{2,1,0:T(8,128)S(1)} fusion(f32[4,16,96]{2,1,0:T(8,128)S(1)} %get-tuple-element.722, s32[]{:T(128)S(6)} %copy.818, bf16[16,30336]{1,0:T(8,128)(2,1)S(1)} %mul.465, bf16[30336,96]{1,0:T(8,128)(2,1)} %get-tuple-element.742), kind=kOutput, calls=%fused_computation.957.clone.1 | convolution fusion | flops 93192192 | bytes 6803460 | tf_op jit(solution)/shard_map/while/body/eval_jaxpr/dot_general | solution.py:194
  419.5 4.4 %fusion.777 = f32[4,16,96]{2,1,0:T(8,128)S(1)} fusion(f32[4,16,96]{2,1,0:T(8,128)S(1)} %get-tuple-element.722, s32[]{:T(128)S(6)} %copy.818, bf16[16,30336]{1,0:T(8,128)(2,1)S(1)} %mul.465, bf16[30336,96]{1,0:T(8,128)(2,1)} %get-tuple-element.742), kind=kOutput, calls=%fused_computation.957.clone.1 | convolution fusion | flops 93192192 | bytes 6803460 | tf_op jit(solution)/shard_map/while/body/eval_jaxpr/dot_general | solution.py:194
  (1899 shorter events, 102.4 us)
Async XLA Ops:
  6.5 6.4 %copy-start = (f32[512,96]{0,1:T(8,128)S(1)}, f32[512,96]{0,1:T(8,128)}, u32[]{:S(2)}) copy-start(f32[512,96]{0,1:T(8,128)} %param.16) | copy-start | bytes 589828
  6.5 178.9 %all-gather.6.cloned.1.call-start = ((), (), s32[]{:S(2)}) async-start(), calls=%async_computation.1 | async-start | bytes 1050624 | tf_op jit(solution)/shard_map/all_gather | solution.py:229
  8.5 12.3 %copy-start.4 = (f32[64,512]{1,0:T(8,128)S(1)}, f32[64,512]{1,0:T(8,128)}, u32[]{:S(2)}) copy-start(f32[64,512]{1,0:T(8,128)} %param.14) | copy-start | bytes 393220
  8.8 20.7 %copy-start.7 = (s32[316]{0:T(512)S(1)}, s32[316]{0:T(512)}, u32[]{:S(2)}) copy-start(s32[316]{0:T(512)} %constant.290) | copy-start | bytes 3796
  9.0 20.7 %copy-start.2 = (f32[96,512]{1,0:T(8,128)S(1)}, f32[96,512]{1,0:T(8,128)}, u32[]{:S(2)}) copy-start(f32[96,512]{1,0:T(8,128)} %param.17) | copy-start | bytes 589828
  9.2 21.3 %copy-start.8 = (bf16[8,316]{1,0:T(8,128)(2,1)S(1)}, bf16[8,316]{1,0:T(8,128)(2,1)}, u32[]{:S(2)}) copy-start(bf16[8,316]{1,0:T(8,128)(2,1)} %constant.269) | copy-start | bytes 15172
  12.1 251.9 %all-gather.4.cloned.1.call-start = ((), (), s32[]{:S(2)}) async-start(), calls=%async_computation | async-start | bytes 7520256 | tf_op jit(solution)/shard_map/all_gather | solution.py:259
  13.1 17.4 %collective-permute-start.1 = (bf16[2,2,2,96]{3,2,1,0:T(2,128)(2,1)S(1)}, bf16[2,2,2,96]{3,2,1,0:T(2,128)(2,1)S(1)}, u32[]{:S(2)}, u32[]{:S(2)}) collective-permute-start(bf16[2,2,2,96]{3,2,1,0:T(2,128)(2,1)S(1)} %bitcast.3837), channel_id=1, source_target_pairs={{64,0},{65,1},{66,2},{67,3},{68,4},{69,5},{70,6},{71,7},{72,8},{73... | collective-permute-start | bytes 4616 | tf_op jit(solution)/shard_map/ppermute | solution.py:26
  14.5 16.1 %collective-permute-start = (bf16[2,2,2,96]{3,2,1,0:T(2,128)(2,1)S(1)}, bf16[2,2,2,96]{3,2,1,0:T(2,128)(2,1)S(1)}, u32[]{:S(2)}, u32[]{:S(2)}) collective-permute-start(bf16[2,2,2,96]{3,2,1,0:T(2,128)(2,1)S(1)} %bitcast.3838), channel_id=1, source_target_pairs={{0,64},{1,65},{2,66},{3,67},{4,68},{5,69},{6,70},{7,71},{8,72},{9,... | collective-permute-start | bytes 4616 | tf_op jit(solution)/shard_map/ppermute | solution.py:26
  21.2 17.3 %collective-permute-start.7 = (bf16[2,4,4,96]{3,2,1,0:T(4,128)(2,1)S(1)}, bf16[2,4,4,96]{3,2,1,0:T(4,128)(2,1)S(1)}, u32[]{:S(2)}, u32[]{:S(2)}) collective-permute-start(bf16[2,4,4,96]{3,2,1,0:T(4,128)(2,1)S(1)} %bitcast.3847), channel_id=1, source_target_pairs={{64,0},{65,1},{66,2},{67,3},{68,4},{69,5},{70,6},{71,7},{72,8},{73... | collective-permute-start | bytes 18440 | tf_op jit(solution)/shard_map/ppermute | solution.py:26
  22.5 16.0 %collective-permute-start.6 = (bf16[2,4,4,96]{3,2,1,0:T(4,128)(2,1)S(1)}, bf16[2,4,4,96]{3,2,1,0:T(4,128)(2,1)S(1)}, u32[]{:S(2)}, u32[]{:S(2)}) collective-permute-start(bf16[2,4,4,96]{3,2,1,0:T(4,128)(2,1)S(1)} %bitcast.3846), channel_id=1, source_target_pairs={{0,64},{1,65},{2,66},{3,67},{4,68},{5,69},{6,70},{7,71},{8,72},{9,... | collective-permute-start | bytes 18440 | tf_op jit(solution)/shard_map/ppermute | solution.py:26
  30.6 13.7 %collective-permute-start.3 = (bf16[6,2,2,96]{3,2,1,0:T(2,128)(2,1)S(1)}, bf16[6,2,2,96]{3,2,1,0:T(2,128)(2,1)S(1)}, u32[]{:S(2)}, u32[]{:S(2)}) collective-permute-start(bf16[6,2,2,96]{3,2,1,0:T(2,128)(2,1)S(1)} %pad_maximum_fusion.3), channel_id=1, source_target_pairs={{8,0},{9,1},{10,2},{11,3},{12,4},{13,5},{14,6},{15,7},{16,8},{17,9... | collective-permute-start | bytes 13832 | tf_op jit(solution)/shard_map/ppermute | solution.py:26
  36.5 7.8 %collective-permute-start.2 = (bf16[6,2,2,96]{3,2,1,0:T(2,128)(2,1)S(1)}, bf16[6,2,2,96]{3,2,1,0:T(2,128)(2,1)S(1)}, u32[]{:S(2)}, u32[]{:S(2)}) collective-permute-start(bf16[6,2,2,96]{3,2,1,0:T(2,128)(2,1)S(1)} %pad_maximum_fusion.3), channel_id=1, source_target_pairs={{0,8},{1,9},{2,10},{3,11},{4,12},{5,13},{6,14},{7,15},{8,16},{9,17... | collective-permute-start | bytes 13832 | tf_op jit(solution)/shard_map/ppermute | solution.py:26
  38.6 15.4 %collective-permute-start.9 = (bf16[8,2,4,96]{3,2,1,0:T(4,128)(2,1)S(1)}, bf16[8,2,4,96]{3,2,1,0:T(4,128)(2,1)S(1)}, u32[]{:S(2)}, u32[]{:S(2)}) collective-permute-start(bf16[8,2,4,96]{3,2,1,0:T(4,128)(2,1)S(1)} %get-tuple-element.335), channel_id=1, source_target_pairs={{8,0},{9,1},{10,2},{11,3},{12,4},{13,5},{14,6},{15,7},{16,8},{17,9... | collective-permute-start | bytes 36872 | tf_op jit(solution)/shard_map/ppermute | solution.py:26
  44.4 23.0 %collective-permute-start.5 = (bf16[6,6,2,96]{3,2,1,0:T(2,128)(2,1)S(1)}, bf16[6,6,2,96]{3,2,1,0:T(2,128)(2,1)S(1)}, u32[]{:S(2)}, u32[]{:S(2)}) collective-permute-start(bf16[6,6,2,96]{3,2,1,0:T(2,128)(2,1)S(1)} %pad_maximum_fusion.2), channel_id=1, source_target_pairs={{1,0},{2,1},{3,2},{4,3},{5,4},{6,5},{7,6},{8,7},{9,8},{10,9},{11,1... | collective-permute-start | bytes 41480 | tf_op jit(solution)/shard_map/ppermute | solution.py:26
  49.3 18.2 %collective-permute-start.4 = (bf16[6,6,2,96]{3,2,1,0:T(2,128)(2,1)S(1)}, bf16[6,6,2,96]{3,2,1,0:T(2,128)(2,1)S(1)}, u32[]{:S(2)}, u32[]{:S(2)}) collective-permute-start(bf16[6,6,2,96]{3,2,1,0:T(2,128)(2,1)S(1)} %pad_maximum_fusion.2), channel_id=1, source_target_pairs={{0,1},{1,2},{2,3},{3,4},{4,5},{5,6},{6,7},{7,8},{8,9},{9,10},{10,1... | collective-permute-start | bytes 41480 | tf_op jit(solution)/shard_map/ppermute | solution.py:26
  51.2 6.6 %collective-permute-start.8 = (bf16[8,2,4,96]{3,2,1,0:T(4,128)(2,1)S(1)}, bf16[8,2,4,96]{3,2,1,0:T(4,128)(2,1)S(1)}, u32[]{:S(2)}, u32[]{:S(2)}) collective-permute-start(bf16[8,2,4,96]{3,2,1,0:T(4,128)(2,1)S(1)} %get-tuple-element.334), channel_id=1, source_target_pairs={{0,8},{1,9},{2,10},{3,11},{4,12},{5,13},{6,14},{7,15},{8,16},{9,17... | collective-permute-start | bytes 36872 | tf_op jit(solution)/shard_map/ppermute | solution.py:26
  58.0 9.6 %collective-permute-start.11 = (bf16[8,8,2,96]{3,2,1,0:T(2,128)(2,1)S(1)}, bf16[8,8,2,96]{3,2,1,0:T(2,128)(2,1)S(1)}, u32[]{:S(2)}, u32[]{:S(2)}) collective-permute-start(bf16[8,8,2,96]{3,2,1,0:T(2,128)(2,1)S(1)} %get-tuple-element.333), channel_id=1, source_target_pairs={{1,0},{2,1},{3,2},{4,3},{5,4},{6,5},{7,6},{8,7},{9,8},{10,9},{11,1... | collective-permute-start | bytes 73736 | tf_op jit(solution)/shard_map/ppermute | solution.py:26
  65.5 8.6 %collective-permute-start.10 = (bf16[8,8,2,96]{3,2,1,0:T(2,128)(2,1)S(1)}, bf16[8,8,2,96]{3,2,1,0:T(2,128)(2,1)S(1)}, u32[]{:S(2)}, u32[]{:S(2)}) collective-permute-start(bf16[8,8,2,96]{3,2,1,0:T(2,128)(2,1)S(1)} %get-tuple-element.332), channel_id=1, source_target_pairs={{0,1},{1,2},{2,3},{3,4},{4,5},{5,6},{6,7},{7,8},{8,9},{9,10},{10,1... | collective-permute-start | bytes 73736 | tf_op jit(solution)/shard_map/ppermute | solution.py:26
  195.5 7.0 %copy-start.1 = (f32[512,1,512]{2,1,0:T(1,128)S(1)}, f32[512,1,512]{2,1,0:T(1,128)}, u32[]{:S(2)}) copy-start(f32[512,1,512]{2,1,0:T(1,128)} %all-gather.6.cloned.1.call-done) | copy-start | bytes 3145732
  300.0 4.5 %copy-start.3 = (f32[96,512]{0,1:T(8,128)S(1)}, f32[96,512]{0,1:T(8,128)}, u32[]{:S(2)}) copy-start(f32[96,512]{0,1:T(8,128)} %copy.132) | copy-start | bytes 589828
  300.0 6.5 %copy-start.6 = (bf16[2,2,2,316]{3,2,1,0:T(2,128)(2,1)S(1)}, bf16[2,2,2,316]{3,2,1,0:T(2,128)(2,1)}, u32[]{:S(2)}) copy-start(bf16[2,2,2,316]{3,2,1,0:T(2,128)(2,1)} %constant.270) | copy-start | bytes 15172
  340.1 1.5 copy-start.5
Sparse Core Ops, SparseCore 0:
  12.2 173.2 all-gather.5
  188.5 75.5 all-gather.3
where the time goes:
time: 440 us; the launch traced here: 432 us
  waiting for transfers between devices  180 us (41%)
  local copies, waits for them, and re-layouts  107 us (24%)
  starting transfers between devices  48.3 us (11%)
  matrix products  44.3 us (10%)
  loops' own time  23.9 us (5%)
  between operations  14.6 us (3%)
  other arithmetic  13.6 us (3%)
    all_gather x1, waiting for transfers between devices, on_device(): everyone = lax.all_gather(own_top, ('oct', 'dev'), axis=0, tiled=True)  111 us
    all_gather x1, waiting for transfers between devices, on_device(): lax.all_gather(part, 'dev', axis=1, tiled=True)  58.1 us
    ppermute x12, starting transfers between devices, from_behind(): lax.ppermute(value, axis, [(source, source + steps) for source in range(i...  48.2 us
    while x1722, local copies, waits for them, and re-layouts  42.4 us
    dot_general x6, matrix products, one_plane(): jnp.dot(stacked.reshape(side_cells * side_cells, -1), weight_rows, prefer...  26.2 us
    another operation x2, loops' own time, plane_rows(): return lax.map(one_plane, jnp.arange(side_cells, dtype=jnp.int32))  23.9 us
    reshape x1, local copies, waits for them, and re-layouts, on_device(): weight_rows = piece.reshape(-1, piece.shape[2])  14.9 us
    mul x24, local copies, waits for them, and re-layouts, one_plane(): stacked = stacked * keep_mask[..., None]  11.6 us
  transfers between devices with their start and end apart: 14, of which 4 were waited for; matrix products, arithmetic and copies ran while one was open for 5% of the time, Pallas kernels for 0%

commit v1 on v0

v1 whole, which is shorter than its diff:
```python
import math

import jax
import jax.numpy as jnp
import numpy as np
from jax import lax
from jax.experimental import pallas as pl
from jax.experimental.pallas import tpu as pltpu
from jax.sharding import PartitionSpec as P


F32 = jnp.float32
BF16 = jnp.bfloat16
MESH = pl.DeviceIdType.MESH
TOPS = 48


def side_maps():
    ids = np.arange(8, dtype=np.float64)
    angles = (2 * ids + 1) * math.pi / 16
    points = np.cos(angles)
    degrees = np.arange(1, 8, dtype=np.float64)
    parent = np.cos(angles[:, None] * degrees[None, :])
    maps = []
    for side in range(2):
        child = np.cos(np.arccos((points + 2 * side - 1) / 2)[:, None] * degrees[None, :])
        maps.append(1 / 8 + 2 / 8 * parent @ child.T)
    return np.stack(maps)


def octant(number):
    return number // 4, number // 2 % 2, number % 2


def tables():
    side = side_maps()
    t = {}
    leaf_order = np.zeros((64, 64))
    up_five = np.zeros((8, 8, 8, 2, 8))
    for box in range(64):
        a, b, c = box // 16, box // 4 % 4, box % 4
        parent = (a // 2) * 4 + (b // 2) * 2 + c // 2
        leaf_order[((b % 2) * 2 + c % 2) * 16 + (a % 2) * 8 + parent, box] = 1
        up_five[:, parent, :, a % 2, parent] = side[a % 2]
    t["leaf_order"] = leaf_order
    pair = np.zeros((2, 2, 8, 8, 8, 8))
    for qy in range(2):
        for qx in range(2):
            pair[qy, qx] = np.einsum("ab,cd->bdac", side[qy], side[qx])
    t["pair_up"] = pair.reshape(256, 64)
    twice = np.stack([side[a // 2] @ side[a % 2] for a in range(4)])
    zmaps, planes = [], []
    for own in range(2):
        upper = np.stack([twice, side[own] @ twice])
        up = np.zeros((2, 4, 8, 8, 2, 8))
        down = np.zeros((2, 8, 8, 128))
        for box in range(8):
            lz, rest = box // 4, box % 4
            for qz in range(2):
                for level in range(2):
                    up[level, rest, :, :, qz, box] = upper[level, 2 * lz + qz]
                    start = 64 + 32 * level + 8 * rest
                    down[qz, :, box, start : start + 8] = upper[level, 2 * lz + qz].T
                for node in range(8):
                    down[qz, :, box, node * 8 + box] = side[qz][node]
        up = np.concatenate([up_five.reshape(64, 128), up.reshape(64, 128)])
        zmaps.append(np.concatenate([halved(up), halved(down.reshape(128, 128))]))
    for own in range(4):
        plane = np.zeros((2, 2, 2, 2, 8, 8, 2, 8, 8))
        for ly, lx, qy, qx in np.ndindex(2, 2, 2, 2):
            first, second = twice[2 * ly + qy], twice[2 * lx + qx]
            plane[ly, lx, qy, qx, :, :, 0] = np.einsum("ab,cd->bdac", first, second)
            plane[ly, lx, qy, qx, :, :, 1] = np.einsum("ab,cd->bdac", side[own // 2] @ first, side[own % 2] @ second)
        planes.append(halved(plane.reshape(1024, 128)))
    t["zmaps"] = np.stack(zmaps)
    t["planes"] = np.stack(planes)
    spread = np.zeros((96, 128))
    for rank in range(96):
        spread[rank, rank // 6 * 8 + rank % 6] = 1
    t["spread"] = spread
    gather = np.zeros((2, 2, 4, 16, 128))
    shift = np.zeros((3, 8, 16, 8, 16))
    lanes = np.zeros((2, 3, 128, 256))
    for pz in range(2):
        for py in range(4):
            for px in range(16):
                source = (py // 2) * 8 + px // 2
                gather[0, pz, py, px, source * 8 + pz * 4 + (py % 2) * 2 + px % 2] = 1
                if py in (0, 3) and px < 8:
                    gather[1, pz, py, px, ((py == 3) * 8 + px) * 8] = 1
    for wx in range(3):
        for px in range(16):
            if 0 <= px + wx - 1 < 16:
                for block in range(8):
                    shift[wx, block, px, block, px + wx - 1] = 1
        for phase in range(8):
            for r in range(8):
                place = phase // 2 * 64 + r * 8 + 1 + 2 * wx + phase % 2
                lanes[0, wx, phase * 8 + r, place] = 1
                lanes[1, wx, 64 + phase * 8 + r, place] = 1
    t["gather"] = np.concatenate([gather.reshape(256, 128), shift.reshape(384, 128)])
    t["lanes"] = lanes.reshape(2, 384, 256)
    sel_three = np.zeros((256, 512))
    for gy in range(2):
        for px in range(4):
            for node in range(1, 7):
                gx = 2 * px - 3 + node
                if 0 <= gx < 8:
                    for r in range(8):
                        sel_three[gy * 128 + 64 + gx * 8 + r, px * 128 + gy * 64 + r * 8 + node] = 1
    t["sel_three"] = sel_three
    sel_two = np.zeros((128, 512))
    for px in range(2):
        for fy in range(2):
            for node in range(1, 7):
                bx = 2 * px - 3 + node
                if 0 <= bx < 4:
                    for r in range(8):
                        sel_two[64 + bx * 8 + r, (px * 2 + fy) * 128 + fy * 64 + r * 8 + node] = 1
    t["sel_two"] = sel_two
    back = np.zeros((16, 16, 256))
    for source in range(16):
        for lp in range(8):
            lz, ly, lx = octant(lp)
            row = lz * 64 + ((source // 8) * 2 + ly) * 16 + (source % 8) * 2 + lx
            back[source, lp, row] = 1
            back[source, 8 + lp, 128 + row] = 1
    t["back"] = back.reshape(256, 256)
    choose = np.zeros((49, 8, 316))
    number = 0
    for cell in range(49):
        for x in range(7):
            if max(abs(cell // 7 - 3), abs(cell % 7 - 3), abs(x - 3)) > 1:
                choose[cell, x, number] = 1
                number += 1
    t["choose"] = choose.reshape(392, 316)
    return t


def top_rows(levels_z):
    table = np.zeros((levels_z // 2, 4, 9, 2, 8, 256))
    for half in range(levels_z // 2):
        for k in range(4):
            for block in range(9):
                for fz in range(2):
                    z = 2 * (half + block // 3 - 1) + fz
                    y = k + block % 3 - 1
                    if 0 <= z < levels_z and 0 <= y < 4:
                        for px in range(4):
                            table[half, k, block, fz, px, px * 32 + z * 4 + y] = 1
                    z = 2 * (half // 2 + block // 3 - 1) + fz
                    for fy in range(2):
                        y = 2 * (k // 2 + block % 3 - 1) + fy
                        if 0 <= z < levels_z // 2 and 0 <= y < 4:
                            for px in range(2):
                                table[half, k, block, fz, 4 + px, 128 + (px * 2 + fy) * 16 + z * 4 + y] = 1
    return table.reshape(levels_z // 2 * 4, 144, 256)[:, :, :192]


def back_tops():
    table = np.zeros((4, 2, 16, 16, 8, TOPS))
    for gz in range(4):
        for k in range(2):
            for source in range(16):
                gy, gx = source // 8, source % 8
                for q in range(8):
                    table[gz, k, source, q, q, gy * 16 + gx] = 1
                table[gz, k, source, 8, gz % 2 * 4 + gy * 2 + gx % 2, 32 + gx // 2] = 1
                table[gz, k, source, 9, gz // 2 * 4 + k * 2 + gx // 2 % 2, 36 + gx // 4] = 1
    return table.reshape(8, 256, 8 * TOPS)


def split(value):
    if isinstance(value, tuple):
        return value
    high = value.astype(BF16)
    return high, (value - high.astype(F32)).astype(BF16)


def fdot(a, b, turned=False):
    (a_high, a_low), (b_high, b_low) = split(a), split(b)
    return bdot(a_high, b_high, turned) + (bdot(a_high, b_low, turned) + bdot(a_low, b_high, turned))


def bdot(a, b, turned=False):
    return lax.dot_general(a, b, (((1,), (1 if turned else 0,)), ((), ())), preferred_element_type=F32)


def rows_to_lanes(value, count):
    rows = value.shape[0] // count
    return jnp.concatenate([value[rows * n : rows * n + rows] for n in range(count)], axis=1)


def lanes_to_rows(value, count):
    width = value.shape[1] // count
    return jnp.concatenate([value[:, width * n : width * n + width] for n in range(count)], axis=0)


def upward(leaves, spread, c):
    order = c("leaf_order")[0]
    parts = [bdot(order, part) for part in split(leaves)]
    mixed = []
    for part in parts:
        lines = []
        for node in range(8):
            lines.append(
                jnp.concatenate([part[16 * n : 16 * n + 16, 64 * node : 64 * node + 64] for n in range(4)], axis=1)
            )
        mixed.append(jnp.concatenate(lines, axis=0).astype(BF16))
    mixed = fdot(c("up"), tuple(mixed))
    four = fdot(mixed[:64], c("pair_up"))
    upper = jnp.concatenate([rows_to_lanes(mixed[64:96], 4), rows_to_lanes(mixed[96:], 4)], axis=0)
    upper = fdot(upper, c("planes"))
    three, two = upper[:8, :64], upper[8:, 64:]
    rest = jnp.concatenate(
        [rows_to_lanes(four, 8), rows_to_lanes(three, 8), rows_to_lanes(two, 8), jnp.zeros((6, 512), F32)], axis=0
    )
    every = [jnp.concatenate([part.astype(BF16), extra], axis=0) for part, extra in zip(parts, split(rest))]
    return fdot(tuple(every), spread, turned=True)


def spread_ranks(turned_compress, c):
    return tuple(bdot(c("spread")[0], part).astype(BF16) for part in split(turned_compress))


def messages(packed, roll):
    tiles = []
    for q in range(8):
        first = q % 4 * 16 + q // 4 * 8
        tiles.append(packed[first : first + 8])
    for q in range(8):
        lines = [packed[64 + q : 65 + q]] + ([packed[72:73], packed[73:74]] if q == 0 else [])
        tiles.append(jnp.concatenate(lines + [jnp.zeros((8 - len(lines), 128), F32)], axis=0))
    lane = lax.broadcasted_iota(jnp.int32, (8, 128), 1)
    for bit in (1, 2, 4, 8):
        upper = lane // 8 // bit % 2 == 1
        for n in range(16):
            if n & bit == 0:
                low, high = tiles[n], tiles[n | bit]
                tiles[n] = jnp.where(upper, roll(high, 8 * bit, 1), low)
                tiles[n | bit] = jnp.where(upper, high, roll(low, 128 - 8 * bit, 1))
    return tiles


def top_row(tiles, roll):
    lane = lax.broadcasted_iota(jnp.int32, (8, 128), 1)
    mask = lane // 8 == 8
    sums = [jnp.zeros((8, 128), F32) for _ in range(3)]
    for n in range(16):
        kept = jnp.where(mask, tiles[n], 0.0)
        gx = n % 8
        sums[n // 8] += roll(kept, 8 * gx, 1) if gx else kept
        sums[2] += roll(kept, 8 * (gx // 2), 1) if gx // 2 else kept
    return jnp.concatenate([sums[0][1:2], sums[1][1:2], sums[2][2:3]], axis=1)


def assemble(received, c):
    picked = bdot(c("gather"), received.astype(BF16))
    lane = lax.broadcasted_iota(jnp.int32, (128, 128), 1)
    return jnp.where(lane < 64, picked[:128], picked[128:]).astype(BF16)


def widen(raw, blocks, five, four, c):
    narrow = jnp.concatenate([raw[z, y] for z, y in blocks], axis=0)
    wide, fours = [], []
    for start in range(0, len(blocks), 8):
        shifted = bdot(c("shift"), narrow[16 * start : 16 * start + 128]).astype(BF16)
        wide.append(rows_to_lanes(shifted, 3))
    wide = jnp.concatenate(wide, axis=0)
    result = bdot(wide, c("lanes_five")).astype(BF16)
    for n, (z, y) in enumerate(blocks):
        five[z, y] = result[16 * n : 16 * n + 16]
        if z in (0, 1, 3) and y in (0, 1, 4, 5):
            fours.append((n, (0, 1, 3).index(z), (0, 1, 4, 5).index(y)))
    result = bdot(jnp.concatenate([wide[16 * n : 16 * n + 16] for n, _, _ in fours], axis=0), c("lanes_four"))
    for place, (_, z, y) in enumerate(fours):
        four[z, y] = result[16 * place : 16 * place + 16].astype(BF16)


OWN = [(z, y) for z in (1, 2) for y in range(1, 5)]
AROUND = [(z, y) for z in range(4) for y in range(6) if (z, y) not in OWN]


def top_blocks(rows, pick, c):
    three = jnp.concatenate([row[:, :256] for row in rows], axis=0).astype(BF16)
    pairs = []
    for n in range(16):
        first = n // 4 * 8 + n % 4
        pairs.append(rows[first][:, 256:] + rows[first + 4][:, 256:])
    two = jnp.concatenate(pairs, axis=0).astype(BF16)
    stacked = jnp.concatenate(
        [
            lanes_to_rows(bdot(three, c("sel_three")), 4),
            lanes_to_rows(bdot(two, c("sel_two")), 4),
        ],
        axis=0,
    ).astype(BF16)
    return bdot(pick, stacked)


def lift_up(summed):
    total = summed[0].astype(F32)
    for n in range(1, 16):
        total = total + summed[n].astype(F32)
    return total


def down_top(summed, expand, c):
    row = lax.broadcasted_iota(jnp.int32, (16, 128), 0)
    scale = jnp.where(row < 8, 0.5, jnp.where(row == 8, 0.25, 0.125))
    fields = fdot((summed * scale)[:, :96], expand)
    two, three = lanes_to_rows(fields[9:10], 8), lanes_to_rows(fields[8:9], 8)
    zero = jnp.zeros((8, 64), F32)
    upper = jnp.concatenate(
        [jnp.concatenate([three, zero], axis=1), jnp.concatenate([zero, two], axis=1)], axis=0
    )
    upper = fdot(upper, c("planes"), turned=True)
    four = fdot(lanes_to_rows(fields[:8], 8), c("pair_up"), turned=True)
    five = fdot(
        c("down"),
        jnp.concatenate([four, lanes_to_rows(upper[:8], 4), lanes_to_rows(upper[8:], 4)], axis=0),
    )
    results = []
    for q in range(8):
        part = five[q // 4 * 64 : q // 4 * 64 + 64, q % 4 * 64 : q % 4 * 64 + 64]
        results.append(rows_to_lanes(part, 8))
    return jnp.concatenate(results, axis=0)


def expand_five(summed, expand):
    parts = []
    for q in range(8):
        pz, lane = q // 4, 128 * (q % 4)
        parts.append(summed[8 * pz : 8 * pz + 8, lane : lane + 128])
    return fdot(jnp.concatenate(parts, axis=0)[:, :96], expand)


def down_five(result, lines, out_ref):
    for q in range(8):
        qz, qy, qx = octant(q)
        for lz in range(2):
            for ly in range(2):
                first = lz * 32 + qz * 16 + ly * 8 + qy * 4 + qx
                source = q * 8 + lz * 4 + ly * 2
                for n in range(4):
                    lines[n, pl.ds(first, 2, stride=2), :] = result[source : source + 2, 128 * n : 128 * n + 128]
    for n in range(4):
        out_ref[:, 128 * n : 128 * n + 128] = lines[n]


PAIRS = {"leaf_order": (64, 64), "spread": (128, 96), "pair_up": (256, 64)}
NARROW = {"lanes_five": 384, "lanes_four": 384, "back": 256}
SELECT = {"sel_three": 256, "sel_two": 128}


def places(sizes):
    start, found = 0, {}
    for name, rows in sizes.items():
        found[name] = start, rows
        start += -(-rows // 16) * 16
    return found, start


PAIR_PLACES, PAIR_ROWS = places({name: shape[0] for name, shape in PAIRS.items()})
NARROW_PLACES, NARROW_ROWS = places(NARROW)
SELECT_PLACES, SELECT_ROWS = places(SELECT)


def halved(value):
    value = value.astype(np.float32)
    high = value.astype(jnp.bfloat16)
    return np.stack([high, (value - high.astype(np.float32)).astype(jnp.bfloat16)])


def packed_tables(groups):
    t = tables()
    t["lanes_five"], t["lanes_four"] = t["lanes"]
    t["spread"] = t["spread"].T
    pairs = np.zeros((PAIR_ROWS, 128))
    for name, (start, rows) in PAIR_PLACES.items():
        pairs[start : start + rows, : PAIRS[name][1]] = t[name]
    narrow = np.zeros((NARROW_ROWS, 256))
    for name, (start, rows) in NARROW_PLACES.items():
        narrow[start : start + rows] = t[name]
    select = np.zeros((SELECT_ROWS, 512))
    for name, (start, rows) in SELECT_PLACES.items():
        select[start : start + rows] = t[name]
    short = lambda value: value.astype(jnp.bfloat16)
    return [
        halved(pairs), short(t["choose"]), short(t["gather"]), short(narrow), short(select),
        t["zmaps"], t["planes"], short(top_rows(groups // 4)), short(back_tops()),
    ]


def getter(pairs, gather, narrow, select, zmaps, planes):
    def get(name):
        if name in ("up", "down"):
            start = 0 if name == "up" else 2
            return zmaps[start], zmaps[start + 1]
        if name == "planes":
            return planes[0], planes[1]
        if name == "gather":
            return gather[0:256]
        if name == "shift":
            return gather[256:640]
        if name in PAIRS:
            start, rows = PAIR_PLACES[name]
            lanes = PAIRS[name][1]
            return tuple(pairs[half, start : start + rows, 0:lanes] for half in range(2))
        if name in NARROW:
            start, rows = NARROW_PLACES[name]
            return narrow[start : start + rows]
        start, rows = SELECT_PLACES[name]
        return select[start : start + rows]

    return get


def place_transfers(m2l, choose, weights, roll):
    for rank in range(0, 8, 2):
        if rank == 6:
            weights[:, 48:64, :] = jnp.zeros((49, 16, 256), BF16)
            continue
        sides = [[], []]
        for n in (rank, rank + 1):
            rows = jnp.concatenate([m2l[n], jnp.zeros((32, 316), BF16)], axis=0)
            low = bdot(choose[0:280, 0:256], rows[:, 0:256], turned=True)
            high = bdot(choose[280:392, 128:316], rows[:, 128:316], turned=True)
            value = jnp.concatenate([low, high], axis=0)
            sides[0].append(value.reshape(49, 8, 128))
            sides[1].append(roll(value, 1, 0).reshape(49, 8, 128))
        for px in range(2):
            both = jnp.concatenate(sides[px], axis=1).astype(BF16)
            weights[:, 8 * rank : 8 * rank + 16, 128 * px : 128 * px + 128] = both


def block_transfers(weights, pz, py, block):
    wz, wy = block // 3, block % 3
    cells = [(2 * wz + fz + 1 - pz) * 7 + 2 * wy + fy + 1 - py for fz in range(2) for fy in range(2)]
    return jnp.concatenate([weights[cell] for cell in cells], axis=0)


def far_tops(four, top_ref, weights, back_top):
    lefts = []
    for block in range(9):
        wz, wy = block // 3, block % 3
        fz_parts = [top_ref[16 * block + 8 * fz : 16 * block + 8 * fz + 8, :] for fz in range(2)]
        tops = jnp.concatenate([jnp.concatenate(fz_parts, axis=1), jnp.zeros((8, 256), F32)], axis=0)
        lefts.append(jnp.concatenate([four[wz, wy : wy + 2].reshape(32, 256), tops.astype(BF16)], axis=0))
    pieces = []
    for child in range(4):
        value = None
        for block in range(9):
            product = bdot(lefts[block], block_transfers(weights, child // 2, child % 2, block))
            value = product if value is None else value + product
        short = value.astype(BF16)
        pieces += [short[:, :128], short[:, 128:]]
    return bdot(back_top, jnp.concatenate(pieces, axis=0)).astype(BF16)


def far_five(five, weights, back, py):
    values = []
    for pz in range(2):
        value = None
        for block in range(9):
            wz, wy = block // 3, block % 3
            left = five[wz : wz + 2, wy : wy + 4].reshape(128, 256)
            product = bdot(left, block_transfers(weights, pz, py, block))
            value = product if value is None else value + product
        values.append(value.astype(BF16))
    return bdot(back, jnp.concatenate(values, axis=0)).astype(BF16)


DIRECTIONS = [(dz, dk) for dz in (-1, 0, 1) for dk in (-1, 0, 1) if (dz, dk) != (0, 0)]


def halo_ranges(step, size):
    if step == 0:
        return pl.ds(1, size), pl.ds(1, size)
    if step == 1:
        return pl.ds(size, 1), pl.ds(0, 1)
    return pl.ds(1, 1), pl.ds(size + 1, 1)


def kernel(groups, *refs):
    sources, out_ref, scratch = refs[:13], refs[13], refs[14:]
    (
        leaf, m2l, compress, expand, pairs, choose, gather, narrow, select, zmaps, planes, pick, back_top,
        weights, message, received, row_ref, raw, five, four, top_ref, reply_top, reply_five, answer_top, answer_five,
        lines, load, send_a, recv_a, send_t, recv_t, send_halo, recv_halo, send_d, recv_d,
    ) = scratch
    o, v = lax.axis_index("oct"), lax.axis_index("dev")
    gz, k, gy, gx = o // 4, o % 4, v // 8, v % 8
    roll = pltpu.roll
    c = getter(pairs, gather, narrow, select, zmaps, planes)

    loads = {}
    for n, target in enumerate(scratch[:13]):
        source = sources[n]
        if target is zmaps:
            source = source.at[gz % 2]
        if target is planes:
            source = source.at[gy % 2 * 2 + gx % 2]
        if target is pick:
            source = source.at[gz // 2 * 4 + k]
        if target is back_top:
            source = source.at[gz % 4 * 2 + k % 2]
        loads[n] = pltpu.make_async_copy(source, target, load.at[n])
    for n in (0, 4, 9, 10, 2):
        loads[n].start()

    raw[...] = jnp.zeros(raw.shape, BF16)
    barrier = pltpu.get_barrier_semaphore()
    layers = groups // 4
    partners = [(n, 0) for n in range(1, layers)] + [(0, n) for n in range(1, 4)]
    partners += [(dz % layers, dk % 4) for dz in (-1, 1) for dk in (-1, 1)]
    for dz, dk in partners:
        target = lax.rem(gz + dz, layers) * 4 + lax.rem(k + dk, 4)
        pl.semaphore_signal(barrier, inc=1, device_id=(target, v), device_id_type=MESH)
    for n in range(1, 16):
        pl.semaphore_signal(barrier, inc=1, device_id=(o, lax.rem(v + n, 16)), device_id_type=MESH)
    for n in (1, 5, 6, 7, 8, 11, 12, 3):
        loads[n].start()

    for n in (0, 4, 9, 10, 2):
        loads[n].wait()
    packed = upward(leaf[...], spread_ranks(compress[...], c), c)
    tiles = messages(packed, roll)
    for n in range(16):
        message[n] = tiles[n]
    received[v] = message[v]
    pl.semaphore_wait(barrier, 15 + len(partners))

    def across(source, target, sems, n):
        return pltpu.make_async_remote_copy(
            src_ref=source.at[lax.rem(v + n, 16)], dst_ref=target.at[v], send_sem=sems[0], recv_sem=sems[1],
            device_id=(o, lax.rem(v + n, 16)), device_id_type=MESH,
        )

    def along_k(n):
        return pltpu.make_async_remote_copy(
            src_ref=row_ref.at[pl.ds(o, 1)], dst_ref=row_ref.at[pl.ds(o, 1)],
            send_sem=send_t.at[0], recv_sem=recv_t.at[0],
            device_id=(gz * 4 + lax.rem(k + n, 4), v), device_id_type=MESH,
        )

    def along_z(n):
        return pltpu.make_async_remote_copy(
            src_ref=row_ref.at[pl.ds(gz * 4, 4)], dst_ref=row_ref.at[pl.ds(gz * 4, 4)],
            send_sem=send_t.at[1], recv_sem=recv_t.at[1],
            device_id=(lax.rem(gz + n, layers) * 4 + k, v), device_id_type=MESH,
        )

    def whole(source, target, count, sems):
        return pltpu.make_async_remote_copy(
            src_ref=source.at[pl.ds(0, count)], dst_ref=target.at[pl.ds(0, count)], send_sem=sems[0], recv_sem=sems[1],
            device_id=(o, lax.rem(v + 1, 16)), device_id_type=MESH,
        )

    sems_a = (send_a, recv_a)
    for n in range(1, 16):
        across(message, received, sems_a, n).start()
    for n in (1, 5, 6, 7, 8, 11, 12, 3):
        loads[n].wait()
    place_transfers(m2l, choose, weights, roll)
    whole(message, received, 15, sems_a).wait_recv()

    got = [received[n] for n in range(16)]
    row_ref[o] = top_row(got, roll)
    for n in range(1, 4):
        along_k(n).start()
    raw[1:3, 1:5] = assemble(jnp.concatenate(got, axis=0), c).reshape(2, 4, 16, 128)

    def halo(number, dz, dk, sign):
        from_z, to_z = halo_ranges(dz, 2)
        from_y, to_y = halo_ranges(dk, 4)
        return pltpu.make_async_remote_copy(
            src_ref=raw.at[from_z, from_y], dst_ref=raw.at[to_z, to_y],
            send_sem=send_halo.at[number], recv_sem=recv_halo.at[number],
            device_id=((gz + sign * dz) * 4 + k + sign * dk, v), device_id_type=MESH,
        )

    def inside(dz, dk):
        return (gz + dz >= 0) & (gz + dz < groups // 4) & (k + dk >= 0) & (k + dk < 4)

    for number, (dz, dk) in enumerate(DIRECTIONS):
        @pl.when(inside(dz, dk))
        def _():
            halo(number, dz, dk, 1).start()

    def rows_of(step):
        return whole(row_ref, row_ref, (3, groups - 4)[step], (send_t.at[step], recv_t.at[step]))

    rows_of(0).wait_recv()
    for n in range(1, layers):
        along_z(n).start()

    widen(raw, OWN, five, four, c)

    for number, (dz, dk) in enumerate(DIRECTIONS):
        @pl.when(inside(-dz, -dk))
        def _():
            halo(number, dz, dk, -1).wait_recv()

    widen(raw, AROUND, five, four, c)
    returned_five = (reply_five, answer_five, (send_d.at[0], recv_d.at[0]))
    returned_top = (reply_top, answer_top, (send_d.at[1], recv_d.at[1]))
    for py in range(2):
        part = far_five(five, weights, c("back"), py).reshape(16, 16, 256)
        reply_five[:, :, 256 * py : 256 * py + 256] = part
    answer_five[v] = reply_five[v]
    for n in range(1, 16):
        across(*returned_five, n).start()

    rows_of(1).wait_recv()
    rows = [row_ref[n] for n in range(groups)]
    top_ref[...] = top_blocks(rows, pick[...], c)
    reply_top[...] = far_tops(four, top_ref, weights, back_top[...]).reshape(16, 16, 128)
    answer_top[v] = reply_top[v]
    for n in range(1, 16):
        across(*returned_top, n).start()

    split_expand = split(expand[...])
    whole(*returned_five[:2], 15, returned_five[2]).wait_recv()
    low = expand_five(lift_up(answer_five), split_expand)
    whole(message, received, 15, sems_a).wait_send()
    for number, (dz, dk) in enumerate(DIRECTIONS):
        @pl.when(inside(dz, dk))
        def _():
            halo(number, dz, dk, 1).wait_send()

    whole(*returned_top[:2], 15, returned_top[2]).wait_recv()
    above = down_top(lift_up(answer_top), split_expand, c)
    down_five(low + above, lines, out_ref)
    for source, target, sems in (returned_five, returned_top):
        whole(source, target, 15, sems).wait_send()
    for step in range(2):
        rows_of(step).wait_send()


def on_device(groups, leaf_multipoles, m2l_ops, compress, expand):
    values = [leaf_multipoles, m2l_ops.transpose(1, 2, 0), compress.T, expand]
    values += [jnp.asarray(value) for value in packed_tables(groups)]
    dma = pltpu.SemaphoreType.DMA
    loaded = [pltpu.VMEM(value.shape, value.dtype) for value in values[:-4]]
    loaded += [pltpu.VMEM(value.shape[1:], value.dtype) for value in values[-4:]]
    return pl.pallas_call(
        lambda *refs: kernel(groups, *refs),
        out_shape=jax.ShapeDtypeStruct((64, 512), F32),
        in_specs=[pl.BlockSpec(memory_space=pltpu.HBM)] * len(values),
        out_specs=pl.BlockSpec(memory_space=pltpu.VMEM),
        scratch_shapes=loaded
        + [
            pltpu.VMEM((49, 64, 256), BF16),
            pltpu.VMEM((16, 8, 128), F32),
            pltpu.VMEM((16, 8, 128), F32),
            pltpu.VMEM((groups, 1, 384), F32),
            pltpu.VMEM((4, 6, 16, 128), BF16),
            pltpu.VMEM((4, 6, 16, 256), BF16),
            pltpu.VMEM((3, 4, 16, 256), BF16),
            pltpu.VMEM((144, 128), F32),
            pltpu.VMEM((16, 16, 128), BF16),
            pltpu.VMEM((16, 16, 512), BF16),
            pltpu.VMEM((16, 16, 128), BF16),
            pltpu.VMEM((16, 16, 512), BF16),
            pltpu.VMEM((4, 64, 128), F32),
            dma((13,)),
            dma, dma, dma((2,)), dma((2,)), dma((8,)), dma((8,)), dma((2,)), dma((2,)),
        ],
        compiler_params=pltpu.CompilerParams(
            collective_id=0, has_side_effects=True, vmem_limit_bytes=60 * 1024 * 1024
        ),
        cost_estimate=pl.CostEstimate(flops=1_000_000_000, bytes_accessed=6_000_000, transcendentals=0),
    )(*values)


def solution(mesh):
    groups = mesh.shape["oct"]
    placed = (P(("oct", "dev"), None), P(None, "dev", None), P(), P())
    return jax.shard_map(
        lambda *args: on_device(groups, *args),
        mesh=mesh, in_specs=placed, out_specs=P(("oct", "dev"), None), check_vma=False,
    )
```

time: 440 us -> 39.1 us (0.09); the launches traced: 432 us -> 38.9 us
  waiting for transfers between devices: 180 us -> 0 us
  local copies, waits for them, and re-layouts: 107 us -> 1.57 us
  starting transfers between devices: 48.3 us -> 0 us
  matrix products: 44.3 us -> 0 us
  Pallas kernels: 0 us -> 37.3 us
  loops' own time: 23.9 us -> 0 us
  between operations: 14.6 us -> 0.01 us
  other arithmetic: 13.6 us -> 0 us
    all_gather x2 -> x0, waiting for transfers between devices: 169 us -> none  [the longest x1 111 us: on_device(): everyone = lax.all_gather(own_top, ('oct', 'dev'), axis=0, tiled=True)]
    while x1723 -> x0, local copies, waits for them, and re-layouts: 52 us -> none
    ppermute x12 -> x0, starting transfers between devices: 48.2 us -> none  [from_behind(): lax.ppermute(value, axis, [(source, source + steps) for source in range(i...]
    dot_general x27 -> x0, matrix products: 44.3 us -> none  [the longest x6 26.2 us: one_plane(): jnp.dot(stacked.reshape(side_cells * side_cells, -1), weight_rows, prefer...]
    pallas_call x0 -> x1, Pallas kernels: none -> 37.3 us  [on_device(): pl.pallas_call(lambda *refs: kernel(groups, *refs), out_shape=jax.ShapeDt...]
    another operation x2 -> x0, loops' own time: 23.9 us -> none  [plane_rows(): return lax.map(one_plane, jnp.arange(side_cells, dtype=jnp.int32))]
    reshape x12 -> x0, local copies, waits for them, and re-layouts: 19 us -> none  [the longest x1 14.9 us: on_device(): weight_rows = piece.reshape(-1, piece.shape[2])]
    mul x28 -> x0, local copies, waits for them, and re-layouts: 12.1 us -> none  [the longest x24 11.6 us: one_plane(): stacked = stacked * keep_mask[..., None]]
  transfers between devices with their start and end apart: 14 -> 0, of which waited for: 4 -> 0; matrix products, arithmetic and copies ran while one was open for 5% -> 0% of each run, Pallas kernels for 0% -> 0%
where the time goes in v1:
time: 39.1 us; the launch traced here: 38.9 us
  Pallas kernels  37.3 us (95%)
  local copies, waits for them, and re-layouts  1.57 us (4%)
    pallas_call x1, Pallas kernels, on_device(): pl.pallas_call(lambda *refs: kernel(groups, *refs), out_shape=jax.ShapeDt...  37.3 us
    unnamed x1, local copies, waits for them, and re-layouts  1.57 us

profile of v1, /device:TPU:1, one launch (start us, length us, event | category | flops | bytes accessed | tf_op | source)
XLA Modules:
  0.0 38.9 jit_solution(6872726621464209647)
XLA Ops:
  0.0 37.3 %shard_map.127 = f32[64,512]{1,0:T(8,128)} custom-call(f32[64,512]{1,0:T(8,128)} %refs_0_.1, bf16[6,96,316]{2,1,0:T(8,128)(2,1)} %bitcast.2, f32[96,512]{1,0:T(8,128)} %bitcast.3, f32[96,512]{1,0:T(8,128)} %refs_3_.1, bf16[2,448,128]{2,1,0:T(8,128)(2,1)} %constant.18.clone.refs_4_, bf16[392,316]{1,0:T(8,128)(2,1)} %constant.19.clone.refs_5_, ...), custom_call_target="tpu_custom_call" | custom-call | flops 1000000000 | bytes 6000000 | tf_op jit(solution)/shard_map/pallas_call | solution.py:647
  37.3 1.6 %copy.15 = f32[64,512]{1,0:T(8,128)} copy(f32[64,512]{1,0:T(8,128)} %shard_map.127) | data formatting | bytes 262144

commit v2 on v1

--- a/solution.py
+++ b/solution.py
@@ -668,7 +668,7 @@
             dma, dma, dma((2,)), dma((2,)), dma((8,)), dma((8,)), dma((2,)), dma((2,)),
         ],
         compiler_params=pltpu.CompilerParams(
-            collective_id=0, has_side_effects=True, vmem_limit_bytes=60 * 1024 * 1024
+            collective_id=0, has_side_effects=True, vmem_limit_bytes=55000 * 1024
         ),
         cost_estimate=pl.CostEstimate(flops=1_000_000_000, bytes_accessed=6_000_000, transcendentals=0),
     )(*values)

time: 39.1 us -> 37.5 us (0.959)
  local copies, waits for them, and re-layouts: 1.57 us -> 0.66 us
  Pallas kernels: 37.3 us -> 36.7 us
    unnamed x1, local copies, waits for them, and re-layouts: 1.57 us -> 0.66 us
    pallas_call x1, Pallas kernels: 37.3 us -> 36.7 us  [on_device(): pl.pallas_call(lambda *refs: kernel(groups, *refs), out_shape=jax.ShapeDt...]
where the time goes in v2:
time: 37.5 us; the launch traced here: 37.4 us
  Pallas kernels  36.7 us (98%)
  local copies, waits for them, and re-layouts  0.66 us (2%)
    pallas_call x1, Pallas kernels, on_device(): pl.pallas_call(lambda *refs: kernel(groups, *refs), out_shape=jax.ShapeDt...  36.7 us

profile of v2, /device:TPU:1, one launch (start us, length us, event | category | flops | bytes accessed | tf_op | source)
XLA Modules:
  0.0 37.4 jit_solution(10654815891564003841)
XLA Ops:
  0.0 36.7 %shard_map.127 = f32[64,512]{1,0:T(8,128)S(1)} custom-call(f32[64,512]{1,0:T(8,128)} %refs_0_.1, bf16[6,96,316]{2,1,0:T(8,128)(2,1)} %bitcast.2, f32[96,512]{1,0:T(8,128)} %bitcast.3, f32[96,512]{1,0:T(8,128)} %refs_3_.1, bf16[2,448,128]{2,1,0:T(8,128)(2,1)} %constant.18.clone.refs_4_, bf16[392,316]{1,0:T(8,128)(2,1)} %constant.19.clone.refs_5_, ...), custom_call_target="tpu_custom_call" | custom-call | flops 1000000000 | bytes 6000000 | tf_op jit(solution)/shard_map/pallas_call | solution.py:647
  36.7 0.7 %copy.15 = f32[64,512]{1,0:T(8,128)} copy(f32[64,512]{1,0:T(8,128)S(1)} %shard_map.127) | data formatting | bytes 262144

commit v3 on v2

--- a/solution.py
+++ b/solution.py
@@ -512,7 +512,7 @@
     raw[...] = jnp.zeros(raw.shape, BF16)
     barrier = pltpu.get_barrier_semaphore()
     layers = groups // 4
-    partners = [(n, 0) for n in range(1, layers)] + [(0, n) for n in range(1, 4)]
+    partners = [(n, 0) for n in sorted(range(1, layers), key=lambda n: abs(n - layers // 2))] + [(0, n) for n in range(1, 4)]
     partners += [(dz % layers, dk % 4) for dz in (-1, 1) for dk in (-1, 1)]
     for dz, dk in partners:
         target = lax.rem(gz + dz, layers) * 4 + lax.rem(k + dk, 4)
@@ -603,14 +603,13 @@
             halo(number, dz, dk, -1).wait_recv()
 
     widen(raw, AROUND, five, four, c)
-    returned_five = (reply_five, answer_five, (send_d.at[0], recv_d.at[0]))
-    returned_top = (reply_top, answer_top, (send_d.at[1], recv_d.at[1]))
+    returned = [(reply_five.at[n], answer_five.at[n], (send_d.at[n], recv_d.at[n])) for n in range(2)]
+    returned_top = (reply_top, answer_top, (send_d.at[2], recv_d.at[2]))
     for py in range(2):
-        part = far_five(five, weights, c("back"), py).reshape(16, 16, 256)
-        reply_five[:, :, 256 * py : 256 * py + 256] = part
-    answer_five[v] = reply_five[v]
-    for n in range(1, 16):
-        across(*returned_five, n).start()
+        reply_five[py] = far_five(five, weights, c("back"), py).reshape(16, 16, 256)
+        answer_five[py, v] = reply_five[py, v]
+        for n in range(1, 16):
+            across(*returned[py], n).start()
 
     rows_of(1).wait_recv()
     rows = [row_ref[n] for n in range(groups)]
@@ -621,8 +620,11 @@
         across(*returned_top, n).start()
 
     split_expand = split(expand[...])
-    whole(*returned_five[:2], 15, returned_five[2]).wait_recv()
-    low = expand_five(lift_up(answer_five), split_expand)
+    halves = []
+    for py in range(2):
+        whole(*returned[py][:2], 15, returned[py][2]).wait_recv()
+        halves.append(lift_up(answer_five.at[py]))
+    low = expand_five(jnp.concatenate(halves, axis=1), split_expand)
     whole(message, received, 15, sems_a).wait_send()
     for number, (dz, dk) in enumerate(DIRECTIONS):
         @pl.when(inside(dz, dk))
@@ -632,7 +634,7 @@
     whole(*returned_top[:2], 15, returned_top[2]).wait_recv()
     above = down_top(lift_up(answer_top), split_expand, c)
     down_five(low + above, lines, out_ref)
-    for source, target, sems in (returned_five, returned_top):
+    for source, target, sems in (*returned, returned_top):
         whole(source, target, 15, sems).wait_send()
     for step in range(2):
         rows_of(step).wait_send()
@@ -660,12 +662,12 @@
             pltpu.VMEM((3, 4, 16, 256), BF16),
             pltpu.VMEM((144, 128), F32),
             pltpu.VMEM((16, 16, 128), BF16),
-            pltpu.VMEM((16, 16, 512), BF16),
+            pltpu.VMEM((2, 16, 16, 256), BF16),
             pltpu.VMEM((16, 16, 128), BF16),
-            pltpu.VMEM((16, 16, 512), BF16),
+            pltpu.VMEM((2, 16, 16, 256), BF16),
             pltpu.VMEM((4, 64, 128), F32),
             dma((13,)),
-            dma, dma, dma((2,)), dma((2,)), dma((8,)), dma((8,)), dma((2,)), dma((2,)),
+            dma, dma, dma((2,)), dma((2,)), dma((8,)), dma((8,)), dma((3,)), dma((3,)),
         ],
         compiler_params=pltpu.CompilerParams(
             collective_id=0, has_side_effects=True, vmem_limit_bytes=55000 * 1024

time: 37.5 us -> 37.4 us (level)
  no operation moved by 1% of the time
where the time goes in v3:
time: 37.4 us; the launch traced here: 37.3 us
  Pallas kernels  36.6 us (98%)
  local copies, waits for them, and re-layouts  0.66 us (2%)
    pallas_call x1, Pallas kernels, on_device(): pl.pallas_call(lambda *refs: kernel(groups, *refs), out_shape=jax.ShapeDt...  36.6 us

profile of v3, /device:TPU:1, one launch (start us, length us, event | category | flops | bytes accessed | tf_op | source)
XLA Modules:
  0.0 37.3 jit_solution(12537426374760867589)
XLA Ops:
  0.0 36.6 %shard_map.127 = f32[64,512]{1,0:T(8,128)S(1)} custom-call(f32[64,512]{1,0:T(8,128)} %refs_0_.1, bf16[6,96,316]{2,1,0:T(8,128)(2,1)} %bitcast.2, f32[96,512]{1,0:T(8,128)} %bitcast.3, f32[96,512]{1,0:T(8,128)} %refs_3_.1, bf16[2,448,128]{2,1,0:T(8,128)(2,1)} %constant.18.clone.refs_4_, bf16[392,316]{1,0:T(8,128)(2,1)} %constant.19.clone.refs_5_, ...), custom_call_target="tpu_custom_call" | custom-call | flops 1000000000 | bytes 6000000 | tf_op jit(solution)/shard_map/pallas_call | solution.py:649
  36.6 0.7 %copy.15 = f32[64,512]{1,0:T(8,128)} copy(f32[64,512]{1,0:T(8,128)S(1)} %shard_map.127) | data formatting | bytes 262144

commit v4 on v3

--- a/solution.py
+++ b/solution.py
@@ -605,12 +605,14 @@
     widen(raw, AROUND, five, four, c)
     returned = [(reply_five.at[n], answer_five.at[n], (send_d.at[n], recv_d.at[n])) for n in range(2)]
     returned_top = (reply_top, answer_top, (send_d.at[2], recv_d.at[2]))
-    for py in range(2):
+
+    def half(py):
         reply_five[py] = far_five(five, weights, c("back"), py).reshape(16, 16, 256)
         answer_five[py, v] = reply_five[py, v]
         for n in range(1, 16):
             across(*returned[py], n).start()
 
+    half(0)
     rows_of(1).wait_recv()
     rows = [row_ref[n] for n in range(groups)]
     top_ref[...] = top_blocks(rows, pick[...], c)
@@ -618,21 +620,22 @@
     answer_top[v] = reply_top[v]
     for n in range(1, 16):
         across(*returned_top, n).start()
+    half(1)
 
     split_expand = split(expand[...])
+    whole(message, received, 15, sems_a).wait_send()
+    for number, (dz, dk) in enumerate(DIRECTIONS):
+        @pl.when(inside(dz, dk))
+        def _():
+            halo(number, dz, dk, 1).wait_send()
+
+    whole(*returned_top[:2], 15, returned_top[2]).wait_recv()
+    above = down_top(lift_up(answer_top), split_expand, c)
     halves = []
     for py in range(2):
         whole(*returned[py][:2], 15, returned[py][2]).wait_recv()
         halves.append(lift_up(answer_five.at[py]))
     low = expand_five(jnp.concatenate(halves, axis=1), split_expand)
-    whole(message, received, 15, sems_a).wait_send()
-    for number, (dz, dk) in enumerate(DIRECTIONS):
-        @pl.when(inside(dz, dk))
-        def _():
-            halo(number, dz, dk, 1).wait_send()
-
-    whole(*returned_top[:2], 15, returned_top[2]).wait_recv()
-    above = down_top(lift_up(answer_top), split_expand, c)
     down_five(low + above, lines, out_ref)
     for source, target, sems in (*returned, returned_top):
         whole(source, target, 15, sems).wait_send()

time: 37.4 us -> 37.6 us (level)
  no operation moved by 1% of the time
where the time goes in v4:
time: 37.6 us; the launch traced here: 37.5 us
  Pallas kernels  36.9 us (98%)
  local copies, waits for them, and re-layouts  0.66 us (2%)
    pallas_call x1, Pallas kernels, on_device(): pl.pallas_call(lambda *refs: kernel(groups, *refs), out_shape=jax.ShapeDt...  36.9 us

profile of v4, /device:TPU:1, one launch (start us, length us, event | category | flops | bytes accessed | tf_op | source)
XLA Modules:
  0.0 37.5 jit_solution(5522634393092322639)
XLA Ops:
  0.0 36.9 %shard_map.127 = f32[64,512]{1,0:T(8,128)S(1)} custom-call(f32[64,512]{1,0:T(8,128)} %refs_0_.1, bf16[6,96,316]{2,1,0:T(8,128)(2,1)} %bitcast.2, f32[96,512]{1,0:T(8,128)} %bitcast.3, f32[96,512]{1,0:T(8,128)} %refs_3_.1, bf16[2,448,128]{2,1,0:T(8,128)(2,1)} %constant.18.clone.refs_4_, bf16[392,316]{1,0:T(8,128)(2,1)} %constant.19.clone.refs_5_, ...), custom_call_target="tpu_custom_call" | custom-call | flops 1000000000 | bytes 6000000 | tf_op jit(solution)/shard_map/pallas_call | solution.py:652
  36.9 0.7 %copy.15 = f32[64,512]{1,0:T(8,128)} copy(f32[64,512]{1,0:T(8,128)S(1)} %shard_map.127) | data formatting | bytes 262144

commit v5 on v4

--- a/solution.py
+++ b/solution.py
@@ -583,17 +583,17 @@
     def inside(dz, dk):
         return (gz + dz >= 0) & (gz + dz < groups // 4) & (k + dk >= 0) & (k + dk < 4)
 
+    def rows_of(step):
+        return whole(row_ref, row_ref, (3, groups - 4)[step], (send_t.at[step], recv_t.at[step]))
+
+    rows_of(0).wait_recv()
+    for n in range(1, layers):
+        along_z(n).start()
+
     for number, (dz, dk) in enumerate(DIRECTIONS):
         @pl.when(inside(dz, dk))
         def _():
             halo(number, dz, dk, 1).start()
-
-    def rows_of(step):
-        return whole(row_ref, row_ref, (3, groups - 4)[step], (send_t.at[step], recv_t.at[step]))
-
-    rows_of(0).wait_recv()
-    for n in range(1, layers):
-        along_z(n).start()
 
     widen(raw, OWN, five, four, c)
 

time: 37.6 us -> 38.4 us (1.021)
  Pallas kernels: 36.9 us -> 37.6 us
    pallas_call x1, Pallas kernels: 36.9 us -> 37.6 us  [on_device(): pl.pallas_call(lambda *refs: kernel(groups, *refs), out_shape=jax.ShapeDt...]
where the time goes in v5:
time: 38.4 us; the launch traced here: 38.3 us
  Pallas kernels  37.6 us (98%)
  local copies, waits for them, and re-layouts  0.66 us (2%)
    pallas_call x1, Pallas kernels, on_device(): pl.pallas_call(lambda *refs: kernel(groups, *refs), out_shape=jax.ShapeDt...  37.6 us

profile of v5, /device:TPU:1, one launch (start us, length us, event | category | flops | bytes accessed | tf_op | source)
XLA Modules:
  0.0 38.3 jit_solution(16840088085336682550)
XLA Ops:
  0.0 37.6 %shard_map.127 = f32[64,512]{1,0:T(8,128)S(1)} custom-call(f32[64,512]{1,0:T(8,128)} %refs_0_.1, bf16[6,96,316]{2,1,0:T(8,128)(2,1)} %bitcast.2, f32[96,512]{1,0:T(8,128)} %bitcast.3, f32[96,512]{1,0:T(8,128)} %refs_3_.1, bf16[2,448,128]{2,1,0:T(8,128)(2,1)} %constant.18.clone.refs_4_, bf16[392,316]{1,0:T(8,128)(2,1)} %constant.19.clone.refs_5_, ...), custom_call_target="tpu_custom_call" | custom-call | flops 1000000000 | bytes 6000000 | tf_op jit(solution)/shard_map/pallas_call | solution.py:652
  37.7 0.7 %copy.15 = f32[64,512]{1,0:T(8,128)} copy(f32[64,512]{1,0:T(8,128)S(1)} %shard_map.127) | data formatting | bytes 262144
